TPU v7x, 256 devices: a whole 4x4x8 slice. The times are simulated.
256 devices in a mesh: dp: 32 (over z, y), tensor: 8 (over x, core).
Axes of the slice: x: 4, y: 4, z: 8, core: 2. Of those that a mesh axis runs over, the one named last changes fastest.
Arguments:
- queries: bfloat16 [4, 3072, 64, 128], P(None, 'dp', 'tensor'), may hold values from -100 to 100
- stored_key_cache: bfloat16 [3072, 8, 48, 128], P('dp', 'tensor'), may hold values from -5 to 5
- stored_value_cache: bfloat16 [3072, 8, 48, 128], P('dp', 'tensor'), may hold values from -6 to 6
- fresh_token_keys: bfloat16 [4, 3072, 8, 128], P(None, 'dp', 'tensor'), may hold values from -6 to 6
- fresh_token_values: bfloat16 [4, 3072, 8, 128], P(None, 'dp', 'tensor'), may hold values from -6 to 6
- request_cache_length: int32 [3072], P('dp'), may hold values from 2 to 48, as said below
- output_projection_weight: bfloat16 [8192, 4096], P('tensor'), may hold values from -0.0625 to 0.0625
- adapter_shrink_weight: bfloat16 [128, 64, 8192], P('dp', None, 'tensor'), may hold values from -0.0625 to 0.0625
- adapter_expand_weight: bfloat16 [128, 64, 4096], P('dp', 'tensor'), may hold values from -0.75 to 0.75
- adapter_place_table: int32 [128], replicated, may hold values from 0 to 127, as said below
- adapter_fetch_table: int32 [1024], P('dp'), may hold values from 0 to 127, as said below
- request_fetch_entry: int32 [3072], P('dp'), may hold values from 0 to 31, as said below
Outputs:
- adapted: bfloat16 [4, 3072, 4096], P(None, 'dp', 'tensor')
Inputs may be any that keep to these rules, and one draw needn't show every extreme that they name: `request_cache_length`: each cached length is 2 or more, and some request holds all 48 positions. `adapter_place_table`: A permutation of the adapter ids. `adapter_fetch_table`: the 32 ids of one index of dp are distinct, and at most 2 of them are stored (adapter_place_table // 4) by one index of dp; every index of dp reaches 2 for some owner. `request_fetch_entry`: every entry of an index's fetch list is used by some of its requests.
All inputs are finite; a program needn't handle non-finite values.
Results may differ from a plain program's by a relative error of at most 0.006.
Values may be sent and summed in bfloat16 or wider, within the bound.
A program may use at most 128 MiB of HBM per device.

v0:
```python
import functools

import jax
import jax.numpy as jnp
from jax import lax
from jax.experimental import pallas as pl
from jax.experimental.pallas import tpu as pltpu
from jax.sharding import PartitionSpec as P

MESH = pl.DeviceIdType.MESH
BF = jnp.bfloat16
F32 = jnp.float32
I32 = jnp.int32

NZ, NY, NX, NT = 8, 4, 4, 8
STEPS, REQ, HEADS, WIDTH, CACHE = 4, 96, 8, 128, 48
ROWS = STEPS * REQ
FEAT = HEADS * WIDTH
RANK, ADP = 64, 4
OUT, SLOTS = 512, 32
PAIRS = REQ // 2
CHUNKS = ((0, 256, 2), (256, 128, 1), (384, 128, 1))
NQ = len(CHUNKS)


def place():
    dp = lax.axis_index("dp")
    t = lax.axis_index("tensor")
    return dp // NY, dp % NY, t


def device(z, y, t):
    return {"dp": z * NY + y, "tensor": t}


def remote(src, dst, send, recv, to):
    return pltpu.make_async_remote_copy(
        src_ref=src, dst_ref=dst, send_sem=send, recv_sem=recv, device_id=to, device_id_type=MESH
    )


def kernel(
    q_hbm, k_hbm, v_hbm, fk_hbm, fv_hbm, len_hbm, wo_hbm, a_hbm, b_hbm, table_hbm, fetch_hbm, entry_hbm,
    o_hbm,
    len_ref, table_ref, fetch_ref, entry_ref, ssem, qv, kv, vv, fkv, fvv, fks, fvs, att, wo, lsem,
    ga, gb0, gb1, gb2, sa, ra, sb, rb, st, rt,
    xg, plr, sx, rx, sp, rp,
    cs, cr, own, xs, xd, sc, rc, sxd, rxd,
    acc, vsh, sh_src, sh_rcv, sh_all, s1, r1, s2, r2,
    ex, fs0, fs1, fs2, fr0, fr1, fr2, rs0, rs1, rs2, rr0, rr1, rr2, ov0, ov1, ov2, fin, sf, rf, sr, rr, osem,
):
    gb = (gb0, gb1, gb2)
    far_src, far_rcv = (fs0, fs1, fs2), (fr0, fr1, fr2)
    ret_src, ret_rcv, ov = (rs0, rs1, rs2), (rr0, rr1, rr2), (ov0, ov1, ov2)
    z, y, t = place()
    x, c = t // 2, t % 2
    up, down = device((z + 1) % NZ, y, t), device((z + NZ - 1) % NZ, y, t)
    yup, ydown = device(z, (y + 1) % NY, t), device(z, (y + NY - 1) % NY, t)

    def y_peer(o):
        return device(z, (y + o) % NY, t)

    def t_peer(o):
        return device(z, y, (t + o) % NT)

    def x_peer(o):
        return device(z, y, ((x + o) % NX) * 2 + c)

    sibling = device(z, y, x * 2 + 1 - c)

    loads = [
        pltpu.make_async_copy(q_hbm, qv, lsem.at[0]),
        pltpu.make_async_copy(k_hbm, kv, lsem.at[1]),
        pltpu.make_async_copy(v_hbm, vv, lsem.at[2]),
        pltpu.make_async_copy(fk_hbm, fkv, lsem.at[3]),
        pltpu.make_async_copy(fv_hbm, fvv, lsem.at[4]),
        pltpu.make_async_copy(a_hbm, ga.at[z], lsem.at[5]),
        pltpu.make_async_copy(wo_hbm, wo, lsem.at[6]),
    ]
    own_b = [
        pltpu.make_async_copy(
            b_hbm.at[:, pl.ds(pl.multiple_of(t * OUT + first, 128), width)],
            gb[q].at[z, pl.ds(pl.multiple_of(t * 32, 32), 32)],
            lsem.at[7 + q],
        )
        for q, (first, width, _) in enumerate(CHUNKS)
    ]
    tables = [
        pltpu.make_async_copy(entry_hbm, entry_ref, ssem.at[0]),
        pltpu.make_async_copy(fetch_hbm, fetch_ref, ssem.at[1]),
        pltpu.make_async_copy(table_hbm, table_ref, ssem.at[2]),
        pltpu.make_async_copy(len_hbm, len_ref, ssem.at[3]),
    ]

    barrier = pltpu.get_barrier_semaphore()
    partners = [up, down] + [y_peer(o) for o in (1, 2, 3)] + [t_peer(o) for o in range(1, NT)]
    for to in partners:
        pl.semaphore_signal(barrier, inc=1, device_id=to, device_id_type=MESH)
    for copy in tables + loads + own_b:
        copy.start()
    pl.semaphore_wait(barrier, len(partners))

    def ring_block(d, k):
        return (z - k + NZ) % NZ if d == 0 else (z + k) % NZ

    def a_copy(d, k, h):
        b = ring_block(d, k)
        part = pl.ds(h * 128, 128)
        src = a_hbm.at[part] if k == 0 else ga.at[b, part]
        return remote(src, ga.at[b, part], sa.at[d, k, h], ra.at[d, k, h], up if d == 0 else down)

    def a_used(d, k, h):
        return k < 3 or h == d

    def a_send(k, h):
        for d in (0, 1):
            if a_used(d, k, h):
                if k > 0:
                    a_copy(d, k - 1, h).wait_recv()
                a_copy(d, k, h).start()

    def b_copy(d, k, q, h=None):
        if CHUNKS[q][2] == 2:
            rows = pl.ds((d if k == 3 else h) * 128, 128)
        else:
            rows = pl.ds(d * 128, 128) if k == 3 else pl.ds(0, 256)
        ref, part = gb[q].at[ring_block(d, k), rows], h or 0
        return remote(ref, ref, sb.at[d, k, q, part], rb.at[d, k, q, part], up if d == 0 else down)

    def b_send(k, q, h=None):
        for d in (0, 1):
            if k > 0:
                b_copy(d, k - 1, q, d if k == 3 and CHUNKS[q][2] == 2 else h).wait_recv()
            b_copy(d, k, q, h).start()

    def b_arrived(q):
        for d in (0, 1):
            if CHUNKS[q][2] == 2:
                b_copy(d, 2, q, 1 - d).wait_recv()
            b_copy(d, 3, q).wait_recv()

    def b_sent(q):
        for d in (0, 1):
            for k in range(4):
                for h in (0, 1) if CHUNKS[q][2] == 2 and k < 3 else (None,):
                    b_copy(d, k, q, h).wait_send()

    def t_copy(o, q):
        first, width, _ = CHUNKS[q]
        return remote(
            b_hbm.at[:, pl.ds(pl.multiple_of(((t + o) % NT) * OUT + first, 128), width)],
            gb[q].at[z, pl.ds(pl.multiple_of(t * 32, 32), 32)],
            st.at[o, q], rt.at[o, q], t_peer(o),
        )

    def t_arrived(o, q):
        b = gb[q].at[z, pl.ds(pl.multiple_of(((t - o + NT) % NT) * 32, 32), 32)]
        remote(b, b, st.at[o, q], rt.at[o, q], t_peer(o)).wait_recv()

    a_send(0, 0)
    a_send(0, 1)
    for q in range(NQ):
        for o in range(1, NT):
            t_copy(o, q).start()

    def place_row(r, carry):
        plr[y, pl.ds(r, 1), :] = jnp.full((1, 128), table_ref[fetch_ref[entry_ref[r]]], I32)
        return carry

    for copy in tables:
        copy.wait()
    lax.fori_loop(0, REQ, place_row, 0, unroll=8)

    def p_copy(o):
        return remote(plr.at[y], plr.at[y], sp.at[o], rp.at[o], y_peer(o))

    def p_arrived(o):
        b = plr.at[(y - o + NY) % NY]
        remote(b, b, sp.at[o], rp.at[o], y_peer(o)).wait_recv()

    for o in (1, 2, 3):
        p_copy(o).start()

    for copy in loads[:5]:
        copy.wait()
    for u in range(STEPS):
        fks[pl.ds(u, REQ, stride=STEPS), :] = fkv[u].astype(F32)
        fvs[pl.ds(u, REQ, stride=STEPS), :] = fvv[u].astype(F32)

    row = lax.broadcasted_iota(I32, (64, 128), 0)
    col = lax.broadcasted_iota(I32, (64, 128), 1)
    row_step, row_req = row // 16, (row // 8) % 2
    cached, fresh = col < 96, (col >= 96) & (col < 104)
    same_cached = cached & ((col // CACHE) == row_req)
    same_fresh = fresh & (((col - 96) // STEPS) == row_req) & (((col - 96) % STEPS) <= row_step)
    position = jnp.where(same_cached, col % CACHE, jnp.where(same_fresh, 0, 1000))
    first = row_req == 0
    scale = WIDTH ** -0.5
    blank = jnp.zeros((24, 128), F32)

    def pair_group(ps):
        count = range(len(ps))
        eights = [pl.ds(pl.multiple_of(p * 8, 8), 8) for p in ps]
        rows = [pl.ds(pl.multiple_of(p * 96, 32), 96) for p in ps]
        sixteens = [pl.ds(pl.multiple_of(p * 16, 16), 16) for p in ps]

        def with_fresh(old, new, i):
            return jnp.concatenate(
                [old[rows[i], :], jnp.concatenate([new[eights[i], :], blank], 0).astype(BF)], 0
            )

        scores = [
            lax.dot_general(
                qv[:, sixteens[i], :].reshape(64, 128), with_fresh(kv, fks, i),
                (((1,), (1,)), ((), ())), preferred_element_type=F32,
            )
            for i in count
        ]
        live = [position < jnp.where(first, len_ref[2 * p], len_ref[2 * p + 1]) for p in ps]
        scores = [jnp.where(live[i], scores[i] * scale, -1e30) for i in count]
        highest = [jnp.max(v, axis=1, keepdims=True) for v in scores]
        powers = [jnp.exp(scores[i] - highest[i]) for i in count]
        sums = [jnp.sum(v, axis=1, keepdims=True) for v in powers]
        weights = [(powers[i] * (1.0 / sums[i])).astype(BF) for i in count]
        results = [
            jnp.dot(weights[i], with_fresh(vv, fvs, i), preferred_element_type=F32) for i in count
        ]
        for i in count:
            att[:, sixteens[i], :] = results[i].reshape(STEPS, 16, 128)

    def pairs(lo, hi, n):
        def some(i, carry):
            pair_group([lo + i * n + j for j in range(n)])
            return carry

        lax.fori_loop(0, (hi - lo) // n, some, 0)

    pairs(0, PAIRS // 2, 4)
    a_send(1, 0)
    pairs(PAIRS // 2, PAIRS, 4)
    for s in range(STEPS):
        for h in range(HEADS):
            xg[y, s * REQ:(s + 1) * REQ, h * WIDTH:(h + 1) * WIDTH] = att[
                s, pl.ds(h, REQ, stride=HEADS), :
            ].astype(BF)

    def x_copy(d, k):
        to = yup if d == 0 else ydown
        if k == 0:
            ref = xg.at[y]
        else:
            ref = xg.at[(y + 3) % NY if d == 0 else (y + 1) % NY, pl.ds(d * (ROWS // 2), ROWS // 2)]
        return remote(ref, ref, sx.at[d, k], rx.at[d, k], to)

    x_copy(0, 0).start()
    x_copy(1, 0).start()
    a_send(1, 1)

    loads[6].wait()

    def weight(i, core):
        return wo[:, pl.ds(pl.multiple_of((i * 2 + core) * OUT, OUT), OUT)]

    def for_sibling(i, carry):
        cs[i] = jnp.dot(xg[y], weight(i, 1 - c), preferred_element_type=F32).astype(BF)
        return carry

    def for_own(i, carry):
        own[i] = jnp.dot(xg[y], weight(i, c), preferred_element_type=F32)
        return carry

    lax.fori_loop(0, NX, for_sibling, 0)
    c_copy = remote(cs, cr, sc.at[0], rc.at[0], sibling)
    c_copy.start()
    lax.fori_loop(0, NX, for_own, 0)
    a_send(2, 0)
    c_copy.wait_recv()

    def xd_copy(o):
        return remote(xs.at[o], xd.at[o], sxd.at[o], rxd.at[o], x_peer(o))

    for o in (2, 1, 3):
        xs[o] = (own[(x + o) % NX] + cr[(x + o) % NX].astype(F32)).astype(BF)
        xd_copy(o).start()
    a_send(2, 1)

    lane = lax.broadcasted_iota(I32, (REQ, 128), 1)

    def index_of(b):
        p = plr[b]
        return jnp.where(((p >> 2) & 3) == y, ((p >> 4) << 2) | (p & 3), -1000)

    def shrink(yb, zb):
        full = lax.dot_general(xg[yb], ga[zb], (((1,), (1,)), ((), ())), preferred_element_type=F32)
        v = vsh[yb]
        lower, upper = v == 4 * zb, v == 4 * zb + 2
        for s in range(STEPS):
            part = full[s * REQ:(s + 1) * REQ]
            acc[yb, s * REQ:(s + 1) * REQ, :] += jnp.where(lower, part[:, :128], 0.0) + jnp.where(
                upper, part[:, 128:], 0.0
            )

    def shrinks(yb, blocks):
        for zb in blocks:
            shrink(yb, zb)

    acc[...] = jnp.zeros_like(acc)
    vsh[y] = index_of(y) - jnp.where(lane >= 64, 1, 0)
    for o in (1, 2, 3):
        p_arrived(o)
        b = (y - o + NY) % NY
        vsh[b] = index_of(b) - jnp.where(lane >= 64, 1, 0)
    loads[5].wait()

    near = [z, (z + 7) % NZ, (z + 1) % NZ]
    far = [(z + 6) % NZ, (z + 2) % NZ]
    last = [(z + 5) % NZ, (z + 3) % NZ]
    shrinks(y, near)
    x_copy(0, 0).wait_recv()
    x_copy(0, 1).start()
    x_copy(1, 0).wait_recv()
    x_copy(1, 1).start()
    a_send(3, 0)
    for q in range(NQ):
        own_b[q].wait()
        for o in range(1, NT):
            t_arrived(o, q)
    shrinks((y + 3) % NY, near)
    shrinks((y + 1) % NY, near)
    a_send(3, 1)
    b_send(0, 0, 0)
    b_send(0, 0, 1)
    b_send(0, 1)
    for yb in (y, (y + 3) % NY, (y + 1) % NY):
        shrinks(yb, far)
    x_copy(0, 1).wait_recv()
    x_copy(1, 1).wait_recv()
    shrinks((y + 2) % NY, near + far)
    a_copy(0, 2, 1).wait_recv()
    a_copy(1, 2, 0).wait_recv()
    for yb in range(NY):
        shrinks(yb, last)
    a_copy(0, 3, 0).wait_recv()
    a_copy(1, 3, 1).wait_recv()
    for yb in range(NY):
        shrinks(yb, [(z + 4) % NZ])

    low = lax.broadcasted_iota(I32, (REQ, 128), 1) < 64
    for b in range(2):
        for s in range(STEPS):
            rows = pl.ds(s * REQ, REQ)
            a0, a1 = acc[b, rows, :], acc[b + 2, rows, :]
            a0 = a0 + pltpu.roll(a0, 64, 1)
            a1 = a1 + pltpu.roll(a1, 64, 1)
            sh_src[b * STEPS + s] = jnp.where(low, a0, a1)

    def s1_copy(o):
        return remote(sh_src.at[(t + o) % NT], sh_rcv.at[o], s1.at[o], r1.at[o], t_peer(o))

    for o in (4, 3, 5, 2, 6, 1, 7):
        s1_copy(o).start()
    b_send(1, 0, 0)
    b_send(1, 0, 1)
    b_send(0, 2)
    fin[...] = own[x] + cr[x].astype(F32)
    for o in (1, 2, 3):
        xd_copy(o).wait_recv()
        fin[...] += xd[o].astype(F32)
    b_send(2, 0, 0)
    b_send(2, 0, 1)
    b_send(1, 1)
    total = sh_src[t]
    for o in range(1, NT):
        s1_copy(o).wait_recv()
        total = total + sh_rcv[o]
    sh_all[t] = total.astype(BF)

    def s2_copy(o):
        return remote(sh_all.at[t], sh_all.at[t], s2.at[o], r2.at[o], t_peer(o))

    def s2_arrived(o):
        b = sh_all.at[(t - o + NT) % NT]
        remote(b, b, s2.at[o], r2.at[o], t_peer(o)).wait_recv()

    for o in (4, 3, 5, 2, 6, 1, 7):
        s2_copy(o).start()
    b_send(3, 0)
    b_send(1, 2)
    for o in range(1, NT):
        s2_arrived(o)

    column = lax.broadcasted_iota(I32, (128, 256), 1)
    spread_row = lax.broadcasted_iota(I32, (128, 256), 0)
    adapter_of = (lax.broadcasted_iota(I32, (REQ, 256), 1) // 8) % ADP

    def spread(yb):
        half = yb // 2
        pick = jnp.where(
            spread_row == half * RANK + (column // 32) * 8 + column % 8, 1.0, 0.0
        ).astype(BF)
        index = index_of(yb)
        v = (jnp.concatenate([index, index], axis=1) - adapter_of).astype(F32).astype(BF)
        for s in range(STEPS):
            wide = jnp.dot(sh_all[(yb % 2) * STEPS + s], pick, preferred_element_type=F32).astype(BF)
            for zb in range(NZ):
                ex[yb, s * REQ:(s + 1) * REQ, zb * 256:(zb + 1) * 256] = jnp.where(
                    v == jnp.asarray(4 * zb, BF), wide, jnp.zeros_like(wide)
                )

    HALF = ROWS // 2
    top, bottom = pl.ds(0, HALF), pl.ds(HALF, HALF)

    def far_copy(d, q):
        return remote(far_src[q].at[d], far_rcv[q].at[d], sf.at[d, q], rf.at[d, q], yup if d == 0 else ydown)

    def ret_copy(d, h, q):
        rows = top if h == 0 else bottom
        return remote(
            ret_src[q].at[d, rows], ret_rcv[q].at[d, rows], sr.at[d, h, q], rr.at[d, h, q], yup if d == 0 else ydown
        )

    def columns(q):
        return slice(CHUNKS[q][0], CHUNKS[q][0] + CHUNKS[q][1])

    def expand(q, o):
        weights = gb[q][...].reshape(NZ * 256, CHUNKS[q][1])
        return jnp.dot(ex[(y + o) % NY], weights, preferred_element_type=F32)

    def give_far(q):
        value = expand(q, 2).astype(BF)
        for d in (0, 1):
            far_src[q][d] = value[d * HALF:(d + 1) * HALF]
            far_copy(d, q).start()

    def give_near(q):
        for d, o in ((0, 1), (1, 3)):
            ret_src[q][d] = expand(q, o).astype(BF)
            ret_copy(d, 1 - d, q).start()

    def pass_on(q):
        for d in (0, 1):
            far_copy(d, q).wait_recv()
            rows = top if d == 0 else bottom
            ret_src[q][d, rows, :] += far_rcv[q][d]
            ret_copy(d, d, q).start()

    def keep(q):
        fin[:, columns(q)] += expand(q, 0)

    spread((y + 2) % NY)
    b_send(2, 1)
    spread((y + 1) % NY)
    spread((y + 3) % NY)
    b_send(2, 2)
    b_arrived(0)
    give_far(0)
    b_send(3, 1)
    give_near(0)
    b_send(3, 2)
    spread(y)
    keep(0)
    pass_on(0)
    b_arrived(1)
    give_far(1)
    give_near(1)
    b_arrived(2)
    give_far(2)
    give_near(2)
    pass_on(1)
    pass_on(2)
    keep(1)
    keep(2)
    writes = []
    for q in range(NQ):
        value = fin[:, columns(q)]
        for d in (0, 1):
            for h in (0, 1):
                ret_copy(d, h, q).wait_recv()
            value = value + ret_rcv[q][d].astype(F32)
        ov[q][...] = value.astype(BF)
        writes.append(pltpu.make_async_copy(ov[q], o_hbm.at[:, columns(q)], osem.at[q]))
        writes[q].start()

    for d in (0, 1):
        for k in range(4):
            for h in range(2):
                if a_used(d, k, h):
                    a_copy(d, k, h).wait_send()
        for k in range(2):
            x_copy(d, k).wait_send()
        for q in range(NQ):
            far_copy(d, q).wait_send()
            for h in (0, 1):
                ret_copy(d, h, q).wait_send()
    for q in range(NQ):
        b_sent(q)
    for o in range(1, NT):
        for q in range(NQ):
            t_copy(o, q).wait_send()
        s1_copy(o).wait_send()
        s2_copy(o).wait_send()
    for o in (1, 2, 3):
        p_copy(o).wait_send()
        xd_copy(o).wait_send()
    c_copy.wait_send()
    for copy in writes:
        copy.wait()


def on_device(q, k, v, fk, fv, lens, wo, a, b, table, fetch, entry):
    vmem, dma = pltpu.VMEM, pltpu.SemaphoreType.DMA
    hbm, smem = pl.BlockSpec(memory_space=pl.ANY), pltpu.SMEM
    widths = [w for _, w, _ in CHUNKS]
    scratch = [
        smem((REQ,), I32), smem((NY * NZ * ADP,), I32), smem((SLOTS,), I32), smem((REQ,), I32), dma((4,)),
        vmem((STEPS, REQ * HEADS, WIDTH), BF), vmem((REQ * CACHE, WIDTH), BF), vmem((REQ * CACHE, WIDTH), BF),
        vmem((STEPS, REQ, WIDTH), BF), vmem((STEPS, REQ, WIDTH), BF),
        vmem((ROWS, WIDTH), F32), vmem((ROWS, WIDTH), F32),
        vmem((STEPS, REQ * HEADS, WIDTH), F32), vmem((FEAT, NT * OUT), BF), dma((7 + NQ,)),
        vmem((NZ, 256, FEAT), BF), *[vmem((NZ, 256, w), BF) for w in widths],
        dma((2, 4, 2)), dma((2, 4, 2)), dma((2, 4, NQ, 2)), dma((2, 4, NQ, 2)), dma((NT, NQ)), dma((NT, NQ)),
        vmem((NY, ROWS, FEAT), BF), vmem((NY, REQ, 128), I32), dma((2, 2)), dma((2, 2)), dma((4,)), dma((4,)),
        vmem((NX, ROWS, OUT), BF), vmem((NX, ROWS, OUT), BF), vmem((NX, ROWS, OUT), F32),
        vmem((NX, ROWS, OUT), BF), vmem((NX, ROWS, OUT), BF), dma((1,)), dma((1,)), dma((4,)), dma((4,)),
        vmem((NY, ROWS, 128), F32), vmem((NY, REQ, 128), I32),
        vmem((NT, REQ, 128), F32), vmem((NT, REQ, 128), F32), vmem((NT, REQ, 128), BF),
        dma((NT,)), dma((NT,)), dma((NT,)), dma((NT,)),
        vmem((NY, ROWS, NZ * 256), BF),
        *[vmem((2, ROWS // 2, w), BF) for w in widths * 2],
        *[vmem((2, ROWS, w), BF) for w in widths * 2],
        *[vmem((ROWS, w), BF) for w in widths],
        vmem((ROWS, OUT), F32), dma((2, NQ)), dma((2, NQ)), dma((2, 2, NQ)), dma((2, 2, NQ)), dma((NQ,)),
    ]
    out = pl.pallas_call(
        kernel,
        out_shape=jax.ShapeDtypeStruct((ROWS, OUT), BF),
        in_specs=[hbm] * 12,
        out_specs=hbm,
        scratch_shapes=scratch,
        compiler_params=pltpu.CompilerParams(
            collective_id=0, has_side_effects=True, vmem_limit_bytes=60 * 2**20
        ),
        name="lora_projection",
    )(
        q.reshape(STEPS, REQ * HEADS, WIDTH),
        k.reshape(REQ * CACHE, WIDTH),
        v.reshape(REQ * CACHE, WIDTH),
        fk.reshape(STEPS, REQ, WIDTH),
        fv.reshape(STEPS, REQ, WIDTH),
        lens,
        wo,
        a.reshape(ADP * RANK, FEAT),
        b.reshape(ADP * 8, NT * OUT),
        table,
        fetch,
        entry,
    )
    return out.reshape(STEPS, REQ, OUT)


def solution(mesh):
    return jax.shard_map(
        on_device,
        mesh=mesh,
        in_specs=(
            P(None, "dp", "tensor", None),
            P("dp", "tensor", None, None),
            P("dp", "tensor", None, None),
            P(None, "dp", "tensor", None),
            P(None, "dp", "tensor", None),
            P("dp"),
            P("tensor", None),
            P("dp", None, "tensor"),
            P("dp", "tensor", None),
            P(),
            P("dp"),
            P("dp"),
        ),
        out_specs=P(None, "dp", "tensor"),
        check_vma=False,
    )
```

profile of v0, /device:TPU:8, one launch (start us, length us, event | category | flops | bytes accessed | tf_op | source)
XLA Modules:
  0.0 89.1 jit_solution(2393702276235186904)
XLA Ops:
  0.0 87.3 %lora_projection.1 = bf16[384,512]{1,0:T(8,128)(2,1)} custom-call(bf16[4,768,128]{2,1,0:T(8,128)(2,1)} %bitcast.11, bf16[4608,128]{1,0:T(8,128)(2,1)} %bitcast.9, bf16[4608,128]{1,0:T(8,128)(2,1)} %bitcast.10, bf16[4,96,128]{2,1,0:T(8,128)(2,1)} %bitcast.14, bf16[4,96,128]{2,1,0:T(8,128)(2,1)} %bitcast.15, s32[96]{0:T(128)} %len_hbm.1, ...), custom_call_target="tpu_custom_call" | custom-call | tf_op jit(solution)/shard_map/lora_projection/pallas_call | solution.py:534
  87.3 1.8 %copy.14 = bf16[4,96,512]{2,1,0:T(8,128)(2,1)} copy(bf16[4,96,512]{2,1,0:T(8,128)(2,1)} %bitcast.8) | data formatting | bytes 786432
where the time goes:
time: 89.2 us; the launch traced here: 89.1 us
  Pallas kernels  87.3 us (98%)
  local copies, waits for them, and re-layouts  1.77 us (2%)
    pallas_call x1, Pallas kernels, on_device(): pl.pallas_call(kernel, out_shape=jax.ShapeDtypeStruct((ROWS, OUT), BF), i...  87.3 us

commit v1 on v0

--- a/solution.py
+++ b/solution.py
@@ -19,7 +19,7 @@
 RANK, ADP = 64, 4
 OUT, SLOTS = 512, 32
 PAIRS = REQ // 2
-CHUNKS = ((0, 256, 2), (256, 128, 1), (384, 128, 1))
+CHUNKS = ((0, 256, 2), (256, 256, 2))
 NQ = len(CHUNKS)
 
 
@@ -43,15 +43,15 @@
     q_hbm, k_hbm, v_hbm, fk_hbm, fv_hbm, len_hbm, wo_hbm, a_hbm, b_hbm, table_hbm, fetch_hbm, entry_hbm,
     o_hbm,
     len_ref, table_ref, fetch_ref, entry_ref, ssem, qv, kv, vv, fkv, fvv, fks, fvs, att, wo, lsem,
-    ga, gb0, gb1, gb2, sa, ra, sb, rb, st, rt,
+    ga, gb0, gb1, sa, ra, sb, rb, st, rt,
     xg, plr, sx, rx, sp, rp,
     cs, cr, own, xs, xd, sc, rc, sxd, rxd,
     acc, vsh, sh_src, sh_rcv, sh_all, s1, r1, s2, r2,
-    ex, fs0, fs1, fs2, fr0, fr1, fr2, rs0, rs1, rs2, rr0, rr1, rr2, ov0, ov1, ov2, fin, sf, rf, sr, rr, osem,
+    ex, fs0, fs1, fr0, fr1, rs0, rs1, rr0, rr1, ov0, ov1, fin, sf, rf, sr, rr, osem,
 ):
-    gb = (gb0, gb1, gb2)
-    far_src, far_rcv = (fs0, fs1, fs2), (fr0, fr1, fr2)
-    ret_src, ret_rcv, ov = (rs0, rs1, rs2), (rr0, rr1, rr2), (ov0, ov1, ov2)
+    gb = (gb0, gb1)
+    far_src, far_rcv = (fs0, fs1), (fr0, fr1)
+    ret_src, ret_rcv, ov = (rs0, rs1), (rr0, rr1), (ov0, ov1)
     z, y, t = place()
     x, c = t // 2, t % 2
     up, down = device((z + 1) % NZ, y, t), device((z + NZ - 1) % NZ, y, t)
@@ -112,8 +112,8 @@
     def a_used(d, k, h):
         return k < 3 or h == d
 
-    def a_send(k, h):
-        for d in (0, 1):
+    def a_send(k, i):
+        for d, h in ((0, i), (1, 1 - i)):
             if a_used(d, k, h):
                 if k > 0:
                     a_copy(d, k - 1, h).wait_recv()
@@ -127,8 +127,9 @@
         ref, part = gb[q].at[ring_block(d, k), rows], h or 0
         return remote(ref, ref, sb.at[d, k, q, part], rb.at[d, k, q, part], up if d == 0 else down)
 
-    def b_send(k, q, h=None):
+    def b_send(k, q, i=None):
         for d in (0, 1):
+            h = i if i is None or d == 0 else 1 - i
             if k > 0:
                 b_copy(d, k - 1, q, d if k == 3 and CHUNKS[q][2] == 2 else h).wait_recv()
             b_copy(d, k, q, h).start()
@@ -316,30 +317,32 @@
     far = [(z + 6) % NZ, (z + 2) % NZ]
     last = [(z + 5) % NZ, (z + 3) % NZ]
     shrinks(y, near)
+    for q in range(NQ):
+        own_b[q].wait()
+        for o in range(1, NT):
+            t_arrived(o, q)
+    b_send(0, 0, 0)
     x_copy(0, 0).wait_recv()
     x_copy(0, 1).start()
     x_copy(1, 0).wait_recv()
     x_copy(1, 1).start()
     a_send(3, 0)
-    for q in range(NQ):
-        own_b[q].wait()
-        for o in range(1, NT):
-            t_arrived(o, q)
+    b_send(0, 0, 1)
+    b_send(0, 1, 0)
     shrinks((y + 3) % NY, near)
     shrinks((y + 1) % NY, near)
-    a_send(3, 1)
-    b_send(0, 0, 0)
-    b_send(0, 0, 1)
-    b_send(0, 1)
     for yb in (y, (y + 3) % NY, (y + 1) % NY):
         shrinks(yb, far)
     x_copy(0, 1).wait_recv()
     x_copy(1, 1).wait_recv()
     shrinks((y + 2) % NY, near + far)
+    b_send(1, 0, 0)
+    b_send(1, 0, 1)
     a_copy(0, 2, 1).wait_recv()
     a_copy(1, 2, 0).wait_recv()
     for yb in range(NY):
         shrinks(yb, last)
+    b_send(1, 1, 0)
     a_copy(0, 3, 0).wait_recv()
     a_copy(1, 3, 1).wait_recv()
     for yb in range(NY):
@@ -352,27 +355,24 @@
             a0, a1 = acc[b, rows, :], acc[b + 2, rows, :]
             a0 = a0 + pltpu.roll(a0, 64, 1)
             a1 = a1 + pltpu.roll(a1, 64, 1)
-            sh_src[b * STEPS + s] = jnp.where(low, a0, a1)
+            sh_src[b * STEPS + s] = jnp.where(low, a0, a1).astype(BF)
 
     def s1_copy(o):
         return remote(sh_src.at[(t + o) % NT], sh_rcv.at[o], s1.at[o], r1.at[o], t_peer(o))
 
     for o in (4, 3, 5, 2, 6, 1, 7):
         s1_copy(o).start()
-    b_send(1, 0, 0)
-    b_send(1, 0, 1)
-    b_send(0, 2)
+    b_send(2, 0, 0)
+    b_send(2, 0, 1)
+    b_send(0, 1, 1)
     fin[...] = own[x] + cr[x].astype(F32)
     for o in (1, 2, 3):
         xd_copy(o).wait_recv()
         fin[...] += xd[o].astype(F32)
-    b_send(2, 0, 0)
-    b_send(2, 0, 1)
-    b_send(1, 1)
-    total = sh_src[t]
+    total = sh_src[t].astype(F32)
     for o in range(1, NT):
         s1_copy(o).wait_recv()
-        total = total + sh_rcv[o]
+        total = total + sh_rcv[o].astype(F32)
     sh_all[t] = total.astype(BF)
 
     def s2_copy(o):
@@ -385,7 +385,8 @@
     for o in (4, 3, 5, 2, 6, 1, 7):
         s2_copy(o).start()
     b_send(3, 0)
-    b_send(1, 2)
+    b_send(2, 1, 0)
+    b_send(1, 1, 1)
     for o in range(1, NT):
         s2_arrived(o)
 
@@ -448,28 +449,21 @@
         fin[:, columns(q)] += expand(q, 0)
 
     spread((y + 2) % NY)
-    b_send(2, 1)
+    b_arrived(0)
+    give_far(0)
     spread((y + 1) % NY)
     spread((y + 3) % NY)
-    b_send(2, 2)
-    b_arrived(0)
-    give_far(0)
     b_send(3, 1)
     give_near(0)
-    b_send(3, 2)
+    b_send(2, 1, 1)
     spread(y)
     keep(0)
     pass_on(0)
     b_arrived(1)
     give_far(1)
     give_near(1)
-    b_arrived(2)
-    give_far(2)
-    give_near(2)
+    keep(1)
     pass_on(1)
-    pass_on(2)
-    keep(1)
-    keep(2)
     writes = []
     for q in range(NQ):
         value = fin[:, columns(q)]
@@ -523,7 +517,7 @@
         vmem((NX, ROWS, OUT), BF), vmem((NX, ROWS, OUT), BF), vmem((NX, ROWS, OUT), F32),
         vmem((NX, ROWS, OUT), BF), vmem((NX, ROWS, OUT), BF), dma((1,)), dma((1,)), dma((4,)), dma((4,)),
         vmem((NY, ROWS, 128), F32), vmem((NY, REQ, 128), I32),
-        vmem((NT, REQ, 128), F32), vmem((NT, REQ, 128), F32), vmem((NT, REQ, 128), BF),
+        vmem((NT, REQ, 128), BF), vmem((NT, REQ, 128), BF), vmem((NT, REQ, 128), BF),
         dma((NT,)), dma((NT,)), dma((NT,)), dma((NT,)),
         vmem((NY, ROWS, NZ * 256), BF),
         *[vmem((2, ROWS // 2, w), BF) for w in widths * 2],

time: 89.2 us -> 87 us (0.975)
  Pallas kernels: 87.3 us -> 85.1 us
    pallas_call x1, Pallas kernels: 87.3 us -> 85.1 us  [on_device(): pl.pallas_call(kernel, out_shape=jax.ShapeDtypeStruct((ROWS, OUT), BF), i...]
where the time goes in v1:
time: 87 us; the launch traced here: 86.9 us
  Pallas kernels  85.1 us (98%)
  local copies, waits for them, and re-layouts  1.77 us (2%)
    pallas_call x1, Pallas kernels, on_device(): pl.pallas_call(kernel, out_shape=jax.ShapeDtypeStruct((ROWS, OUT), BF), i...  85.1 us
    unnamed x1, local copies, waits for them, and re-layouts  1.77 us

profile of v1, /device:TPU:8, one launch (start us, length us, event | category | flops | bytes accessed | tf_op | source)
XLA Modules:
  0.0 86.9 jit_solution(6679060714246299264)
XLA Ops:
  0.0 85.1 %lora_projection.1 = bf16[384,512]{1,0:T(8,128)(2,1)} custom-call(bf16[4,768,128]{2,1,0:T(8,128)(2,1)} %bitcast.11, bf16[4608,128]{1,0:T(8,128)(2,1)} %bitcast.9, bf16[4608,128]{1,0:T(8,128)(2,1)} %bitcast.10, bf16[4,96,128]{2,1,0:T(8,128)(2,1)} %bitcast.14, bf16[4,96,128]{2,1,0:T(8,128)(2,1)} %bitcast.15, s32[96]{0:T(128)} %len_hbm.1, ...), custom_call_target="tpu_custom_call" | custom-call | tf_op jit(solution)/shard_map/lora_projection/pallas_call | solution.py:528
  85.1 1.8 %copy.14 = bf16[4,96,512]{2,1,0:T(8,128)(2,1)} copy(bf16[4,96,512]{2,1,0:T(8,128)(2,1)} %bitcast.8) | data formatting | bytes 786432

commit v2 on v1

--- a/solution.py
+++ b/solution.py
@@ -47,7 +47,7 @@
     xg, plr, sx, rx, sp, rp,
     cs, cr, own, xs, xd, sc, rc, sxd, rxd,
     acc, vsh, sh_src, sh_rcv, sh_all, s1, r1, s2, r2,
-    ex, fs0, fs1, fr0, fr1, rs0, rs1, rr0, rr1, ov0, ov1, fin, sf, rf, sr, rr, osem,
+    ex, fs0, fs1, fr0, fr1, rs0, rs1, rr0, rr1, ov0, ov1, fin, farx, sf, rf, sr, rr, osem,
 ):
     gb = (gb0, gb1)
     far_src, far_rcv = (fs0, fs1), (fr0, fr1)
@@ -345,23 +345,29 @@
     b_send(1, 1, 0)
     a_copy(0, 3, 0).wait_recv()
     a_copy(1, 3, 1).wait_recv()
-    for yb in range(NY):
-        shrinks(yb, [(z + 4) % NZ])
-
     low = lax.broadcasted_iota(I32, (REQ, 128), 1) < 64
+
+    def s1_copy(o):
+        return remote(sh_src.at[(t + o) % NT], sh_rcv.at[o], s1.at[o], r1.at[o], t_peer(o))
+
+    def give_share(j):
+        o = (j - t + NT) % NT
+
+        @pl.when(o != 0)
+        def _():
+            s1_copy(o).start()
+
     for b in range(2):
+        shrinks(b, [(z + 4) % NZ])
+        shrinks(b + 2, [(z + 4) % NZ])
         for s in range(STEPS):
             rows = pl.ds(s * REQ, REQ)
             a0, a1 = acc[b, rows, :], acc[b + 2, rows, :]
             a0 = a0 + pltpu.roll(a0, 64, 1)
             a1 = a1 + pltpu.roll(a1, 64, 1)
             sh_src[b * STEPS + s] = jnp.where(low, a0, a1).astype(BF)
-
-    def s1_copy(o):
-        return remote(sh_src.at[(t + o) % NT], sh_rcv.at[o], s1.at[o], r1.at[o], t_peer(o))
-
-    for o in (4, 3, 5, 2, 6, 1, 7):
-        s1_copy(o).start()
+        for s in range(STEPS):
+            give_share(b * STEPS + s)
     b_send(2, 0, 0)
     b_send(2, 0, 1)
     b_send(0, 1, 1)
@@ -427,8 +433,15 @@
         weights = gb[q][...].reshape(NZ * 256, CHUNKS[q][1])
         return jnp.dot(ex[(y + o) % NY], weights, preferred_element_type=F32)
 
-    def give_far(q):
-        value = expand(q, 2).astype(BF)
+    def expand_block(q, o, zb):
+        cols = pl.ds(pl.multiple_of(zb * 256, 256), 256)
+        return jnp.dot(ex[(y + o) % NY, :, cols], gb[q][zb], preferred_element_type=F32)
+
+    def give_far(q, early=None):
+        if early is None:
+            value = expand(q, 2).astype(BF)
+        else:
+            value = (early[...] + expand_block(q, 2, (z + 4) % NZ)).astype(BF)
         for d in (0, 1):
             far_src[q][d] = value[d * HALF:(d + 1) * HALF]
             far_copy(d, q).start()
@@ -459,8 +472,14 @@
     spread(y)
     keep(0)
     pass_on(0)
-    b_arrived(1)
-    give_far(1)
+    for d in (0, 1):
+        b_copy(d, 2, 1, 1 - d).wait_recv()
+    farx[...] = expand_block(1, 2, z)
+    for i in (1, 2, 3, 5, 6, 7):
+        farx[...] += expand_block(1, 2, (z + i) % NZ)
+    for d in (0, 1):
+        b_copy(d, 3, 1).wait_recv()
+    give_far(1, farx)
     give_near(1)
     keep(1)
     pass_on(1)
@@ -523,7 +542,7 @@
         *[vmem((2, ROWS // 2, w), BF) for w in widths * 2],
         *[vmem((2, ROWS, w), BF) for w in widths * 2],
         *[vmem((ROWS, w), BF) for w in widths],
-        vmem((ROWS, OUT), F32), dma((2, NQ)), dma((2, NQ)), dma((2, 2, NQ)), dma((2, 2, NQ)), dma((NQ,)),
+        vmem((ROWS, OUT), F32), vmem((ROWS, CHUNKS[1][1]), F32), dma((2, NQ)), dma((2, NQ)), dma((2, 2, NQ)), dma((2, 2, NQ)), dma((NQ,)),
     ]
     out = pl.pallas_call(
         kernel,

time: 87 us -> 86.8 us (level)
  no operation moved by 1% of the time
where the time goes in v2:
time: 86.8 us; the launch traced here: 86.7 us
  Pallas kernels  84.9 us (98%)
  local copies, waits for them, and re-layouts  1.77 us (2%)
    pallas_call x1, Pallas kernels, on_device(): pl.pallas_call(kernel, out_shape=jax.ShapeDtypeStruct((ROWS, OUT), BF), i...  84.9 us
    unnamed x1, local copies, waits for them, and re-layouts  1.77 us

profile of v2, /device:TPU:8, one launch (start us, length us, event | category | flops | bytes accessed | tf_op | source)
XLA Modules:
  0.0 86.7 jit_solution(3333125733100935745)
XLA Ops:
  0.0 84.9 %lora_projection.1 = bf16[384,512]{1,0:T(8,128)(2,1)} custom-call(bf16[4,768,128]{2,1,0:T(8,128)(2,1)} %bitcast.11, bf16[4608,128]{1,0:T(8,128)(2,1)} %bitcast.9, bf16[4608,128]{1,0:T(8,128)(2,1)} %bitcast.10, bf16[4,96,128]{2,1,0:T(8,128)(2,1)} %bitcast.14, bf16[4,96,128]{2,1,0:T(8,128)(2,1)} %bitcast.15, s32[96]{0:T(128)} %len_hbm.1, ...), custom_call_target="tpu_custom_call" | custom-call | tf_op jit(solution)/shard_map/lora_projection/pallas_call | solution.py:547
  84.9 1.8 %copy.14 = bf16[4,96,512]{2,1,0:T(8,128)(2,1)} copy(bf16[4,96,512]{2,1,0:T(8,128)(2,1)} %bitcast.8) | data formatting | bytes 786432
